TPU v7x, 32 devices: a whole 2x2x4 slice. The times are simulated.
32 devices in a mesh: layer: 4 (over y, x), feat: 8 (over z, core).
Axes of the slice: x: 2, y: 2, z: 4, core: 2. Of those that a mesh axis runs over, the one named last changes fastest.
Arguments:
- source_decoder: bfloat16 [4, 1024, 8192], P('layer', 'feat'), may hold values from -0.0625 to 0.0625
- reader_encoder: bfloat16 [4, 8192, 6144], P('layer', None, 'feat'), may hold values from -6 to 6
- source_acts: bfloat16 [2048, 4096], P('feat', 'layer'), may hold values from 0 to 2
- target_grads: bfloat16 [2048, 24576], P('feat', 'layer'), may hold values from -0.13183594 to 0.13183594
- pair_source: int32 [4, 8, 24], P('layer', 'feat'), may hold values from 0 to 3
- pair_target: int32 [4, 8, 24], P('layer', 'feat'), may hold values from 0 to 5
- pair_count: int32 [4, 8], P('layer', 'feat'), may hold values from 1 to 24, as said below
Outputs:
- edge_table: float32 [4, 8, 24, 128, 128], P('layer', 'feat')
Inputs may be any that keep to these rules, and one draw needn't show every extreme that they name: `pair_count`: slots at and past the count of a reader layer and column are unused; in every draw some reader layer and column uses all 24 slots.
All inputs are finite; a program needn't handle non-finite values.
Results may differ from a plain program's by a relative error of at most 0.0003.
Values may be sent and summed in bfloat16 or wider, within the bound.
A program may use at most 192 MiB of HBM per device.

v0:
```python
import jax
import jax.numpy as jnp
from jax import lax
from jax.sharding import PartitionSpec as P


def local(
    source_decoder, reader_encoder, source_acts, target_grads, pair_source, pair_target, pair_count
):
    source_rows, target_rows = (
        lax.all_to_all(source_acts, "feat", split_axis=1, concat_axis=0, tiled=True),
        lax.all_to_all(target_grads, "feat", split_axis=1, concat_axis=0, tiled=True),
    )
    encoder = reader_encoder[0]
    block_size = source_decoder.shape[1]
    source_slab = source_rows[None]
    sources = pair_source[0, 0]
    targets = pair_target[0, 0]
    slot_count = sources.shape[0]
    live_count = pair_count[0, 0]
    panel_dec, panel_act = (
        lax.all_gather(source_decoder, "layer", axis=0, tiled=True),
        lax.all_gather(source_slab, "layer", axis=0, tiled=True),
    )

    def one_pair(slot_pos, edge_buffer):
        source = sources[slot_pos]
        target = targets[slot_pos]
        decoder_block = lax.dynamic_index_in_dim(panel_dec, source, 0, keepdims=False)
        enc_block = lax.dynamic_slice_in_dim(encoder, target * block_size, block_size, 1)
        virtual = jnp.dot(decoder_block, enc_block, preferred_element_type=jnp.float32)
        act_block = lax.dynamic_index_in_dim(panel_act, source, 0, keepdims=False)
        grad_block = lax.dynamic_slice_in_dim(target_rows, target * block_size, block_size, 1)
        coact = lax.dot_general(
            act_block, grad_block, (((0,), (0,)), ((), ())), preferred_element_type=jnp.float32
        )
        return lax.dynamic_update_index_in_dim(edge_buffer, virtual * coact, slot_pos, 0)

    edge_table = lax.fori_loop(
        0, live_count, one_pair, jnp.zeros((slot_count, block_size, block_size), jnp.float32)
    )
    return edge_table[None, None]


def solution(mesh):
    in_specs = (
        P("layer", "feat", None),
        P("layer", None, "feat"),
        P("feat", "layer"),
        P("feat", "layer"),
        P("layer", "feat", None),
        P("layer", "feat", None),
        P("layer", "feat"),
    )
    out_specs = P("layer", "feat", None, None, None)
    return jax.shard_map(local, mesh=mesh, in_specs=in_specs, out_specs=out_specs, check_vma=False)
```

profile of v0, /device:TPU:5, one launch (start us, length us, event | category | flops | bytes accessed | tf_op | source)
XLA Modules:
  0.0 375.2 jit_solution(6197434539734011829)
XLA Ops:
  6.5 1.0 copy-done
  7.7 19.8 %all_to_all.35 = bf16[256,8,128]{2,0,1:T(8,128)(2,1)} all-to-all(bf16[256,8,128]{2,0,1:T(8,128)(2,1)S(1)} %copy_bitcast_fusion.1), channel_id=1, replica_groups=mesh['layer'=4,'feat'=8] {'feat'}, dimensions={1} | all-to-all | bytes 1048576 | tf_op jit(solution)/shard_map/all_to_all | solution.py:11
  27.5 0.7 all-gather.3.cloned.1.call-update
  28.2 3.8 %copy.16 = bf16[32,8,8,768]{3,2,0,1:T(8,128)(2,1)} copy(bf16[32,8,8,768]{3,2,1,0:T(8,128)(2,1)} %bitcast.44) | data formatting | bytes 6291456 | tf_op jit(solution)/shard_map/all_to_all | solution.py:12
  32.1 5.5 %all-to-all-start.1 = ((bf16[256,8,768]{2,0,1:T(8,128)(2,1)}), bf16[256,8,768]{2,0,1:T(8,128)(2,1)}, u32[]{:S(2)}, u32[]{:S(2)}) async-start(bf16[256,8,768]{2,0,1:T(8,128)(2,1)} %bitcast.42), calls=%async_computation.1 | async-start | bytes 6291456 | tf_op jit(solution)/shard_map/all_to_all | solution.py:12
  37.6 24.6 %all-gather.5.cloned.1.call-done = bf16[4,2048,128]{2,1,0:T(8,128)(2,1)} async-done(((bf16[1,2048,128]{2,1,0:T(8,128)(2,1)}), bf16[4,2048,128]{2,1,0:T(8,128)(2,1)}) %all-gather.5.cloned.1.call-update) | async-done | bytes 2097168 | tf_op jit(solution)/shard_map/all_gather | solution.py:23
  62.2 46.2 %all-to-all-done.1 = bf16[256,8,768]{2,0,1:T(8,128)(2,1)} async-done(((bf16[256,8,768]{2,0,1:T(8,128)(2,1)}), bf16[256,8,768]{2,0,1:T(8,128)(2,1)}, u32[]{:S(2)}, u32[]{:S(2)}) %all-to-all-start.1) | async-done | bytes 3145760 | tf_op jit(solution)/shard_map/all_to_all | solution.py:12
  108.4 43.3 %all-gather.3.cloned.1.call-done = bf16[4,128,8192]{2,1,0:T(8,128)(2,1)} async-done(((bf16[1,128,8192]{2,1,0:T(8,128)(2,1)}), bf16[4,128,8192]{2,1,0:T(8,128)(2,1)}) %all-gather.3.cloned.1.call-update) | async-done | bytes 8388624 | tf_op jit(solution)/shard_map/all_gather | solution.py:22
  151.8 215.3 %while.10 = (s32[]{:T(128)}, f32[24,128,128]{2,1,0:T(8,128)S(1)}, s32[]{:T(128)}, s32[24]{0:T(128)S(1)}, bf16[4,128,8192]{2,1,0:T(8,128)(2,1)}, /*index=5*/s32[2...) while((s32[]{:T(128)}, f32[24,128,128]{2,1,0:T(8,128)S(1)}, ...), condition=%wide.region_1.2_spmd, body=%wide.region_0.1_spmd.sunk | while | flops 335560704 | bytes 5439787 | solution.py:39
  155.0 0.7 dynamic_slice.42
  156.3 2.9 fusion.22
  159.2 1.5 fusion.23
  164.0 0.7 dynamic_slice.42
  165.2 2.9 fusion.22
  168.2 1.6 fusion.23
  173.0 0.7 dynamic_slice.42
  174.2 2.9 fusion.22
  177.2 1.5 fusion.23
  181.9 0.7 dynamic_slice.42
  183.2 2.9 fusion.22
  186.1 1.5 fusion.23
  190.8 0.7 dynamic_slice.42
  192.1 2.9 fusion.22
  195.0 1.5 fusion.23
  199.8 0.7 dynamic_slice.42
  201.1 2.9 fusion.22
  204.0 1.5 fusion.23
  210.0 2.9 fusion.22
  212.9 1.5 fusion.23
  218.9 2.9 fusion.22
  221.9 1.5 fusion.23
  227.9 2.9 fusion.22
  230.8 1.5 fusion.23
  236.8 2.9 fusion.22
  239.8 1.5 fusion.23
  245.8 2.9 fusion.22
  248.7 1.5 fusion.23
  254.7 2.9 fusion.22
  257.7 1.5 fusion.23
  263.7 2.9 fusion.22
  266.6 1.5 fusion.23
  272.6 2.9 fusion.22
  275.5 1.5 fusion.23
  281.6 2.9 fusion.22
  284.5 1.5 fusion.23
  290.5 2.9 fusion.22
  293.4 1.5 fusion.23
  299.4 2.9 fusion.22
  302.4 1.5 fusion.23
  308.4 2.9 fusion.22
  311.3 1.5 fusion.23
  317.3 2.9 fusion.22
  320.3 1.5 fusion.23
  326.3 2.9 fusion.22
  329.2 1.5 fusion.23
  335.2 2.9 fusion.22
  338.1 1.5 fusion.23
  344.2 2.9 fusion.22
  347.1 1.5 fusion.23
  353.1 2.9 fusion.22
  356.0 1.5 fusion.23
  362.0 2.9 fusion.22
  365.0 1.5 fusion.23
  367.2 1.1 copy-done.1
  (53 shorter events, 27.6 us)
Async XLA Ops:
  6.5 1.0 copy-start
  6.5 55.6 %all-gather.5.cloned.1.call-start = ((), (), s32[]{:S(2)}) async-start(), calls=%async_computation.3 | async-start | bytes 2621440 | tf_op jit(solution)/shard_map/all_gather | solution.py:23
  27.5 124.2 %all-gather.3.cloned.1.call-start = ((), (), s32[]{:S(2)}) async-start(), calls=%async_computation.2 | async-start | bytes 10485760 | tf_op jit(solution)/shard_map/all_gather | solution.py:22
  32.0 119.8 %copy-start.2 = (s32[1,1,24]{2,1,0:T(1,128)S(1)}, s32[1,1,24]{2,1,0:T(1,128)}, u32[]{:S(2)}) copy-start(s32[1,1,24]{2,1,0:T(1,128)} %param.13) | copy-start | bytes 292
  32.1 119.8 %copy-start.3 = (s32[1,1,24]{2,1,0:T(1,128)S(1)}, s32[1,1,24]{2,1,0:T(1,128)}, u32[]{:S(2)}) copy-start(s32[1,1,24]{2,1,0:T(1,128)} %param.14) | copy-start | bytes 292
  32.1 76.3 %all-to-all-start.1 = ((bf16[256,8,768]{2,0,1:T(8,128)(2,1)}), bf16[256,8,768]{2,0,1:T(8,128)(2,1)}, u32[]{:S(2)}, u32[]{:S(2)}) async-start(bf16[256,8,768]{2,0,1:T(8,128)(2,1)} %bitcast.42), calls=%async_computation.1 | async-start | bytes 6291456 | tf_op jit(solution)/shard_map/all_to_all | solution.py:12
  367.2 1.1 copy-start.1
Sparse Core Ops, SparseCore 0:
  27.6 34.5 all-gather.4
  64.0 87.5 all-gather.2
where the time goes:
time: 377 us; the launch traced here: 375 us
  waiting for transfers between devices  115 us (31%)
  matrix products  107 us (28%)
  loops' own time  76.8 us (20%)
  local copies, waits for them, and re-layouts  37.4 us (10%)
  blocking collectives  19.8 us (5%)
  between operations  13.5 us (4%)
  starting transfers between devices  5.58 us (1%)
    another operation x1, loops' own time, local(): lax.fori_loop(0, live_count, one_pair, jnp.zeros((slot_count, block_size,...  76.8 us
    dot_general x24, matrix products, one_pair(): jnp.dot(decoder_block, enc_block, preferred_element_type=jnp.float32)  70.2 us
    all_to_all x1, waiting for transfers between devices, local(): lax.all_to_all(target_grads, 'feat', split_axis=1, concat_axis=0, tiled=T...  46.2 us
    all_gather x1, waiting for transfers between devices, local(): lax.all_gather(source_decoder, 'layer', axis=0, tiled=True)  43.3 us
    dot_general x24, matrix products, one_pair(): lax.dot_general(act_block, grad_block, (((0,), (0,)), ((), ())), preferre...  37.2 us
    all_gather x1, waiting for transfers between devices, local(): lax.all_gather(source_slab, 'layer', axis=0, tiled=True)  24.6 us
    all_to_all x1, blocking collectives, local(): lax.all_to_all(source_acts, 'feat', split_axis=1, concat_axis=0, tiled=True)  19.8 us
    dynamic_slice x24, local copies, waits for them, and re-layouts, one_pair(): target = targets[slot_pos]  15.6 us
  transfers between devices with their start and end apart: 3, of which 3 were waited for; matrix products, arithmetic and copies ran while one was open for 1% of the time, Pallas kernels for 0%

commit v1 on v0

--- a/solution.py
+++ b/solution.py
@@ -8,7 +8,12 @@
     source_decoder, reader_encoder, source_acts, target_grads, pair_source, pair_target, pair_count
 ):
     source_rows, target_rows = (
-        lax.all_to_all(source_acts, "feat", split_axis=1, concat_axis=0, tiled=True),
+        jnp.concatenate(
+            lax.all_to_all(
+                jnp.stack(jnp.split(source_acts, lax.axis_size("feat"), axis=1)), "feat", 0, 0
+            ),
+            axis=0,
+        ),
         lax.all_to_all(target_grads, "feat", split_axis=1, concat_axis=0, tiled=True),
     )
     encoder = reader_encoder[0]

time: 377 us -> 386 us (1.024)
  matrix products: 107 us -> 119 us
  loops' own time: 76.8 us -> 70.9 us
    dot_general x24, matrix products: 37.2 us -> 48.6 us  [one_pair(): lax.dot_general(act_block, grad_block, (((0,), (0,)), ((), ())), preferre...]
    another operation x1, loops' own time: 76.8 us -> 70.9 us  [local(): lax.fori_loop(0, live_count, one_pair, jnp.zeros((slot_count, block_size,...]
    unnamed x8 -> x13, local copies, waits for them, and re-layouts: 2.18 us -> 6.13 us
where the time goes in v1:
time: 386 us; the launch traced here: 384 us
  matrix products  119 us (31%)
  waiting for transfers between devices  117 us (30%)
  loops' own time  70.9 us (18%)
  local copies, waits for them, and re-layouts  38.4 us (10%)
  blocking collectives  19.8 us (5%)
  between operations  13.4 us (3%)
  starting transfers between devices  4.78 us (1%)
    another operation x1, loops' own time, local(): lax.fori_loop(0, live_count, one_pair, jnp.zeros((slot_count, block_size,...  70.9 us
    dot_general x24, matrix products, one_pair(): jnp.dot(decoder_block, enc_block, preferred_element_type=jnp.float32)  70.2 us
    dot_general x24, matrix products, one_pair(): lax.dot_general(act_block, grad_block, (((0,), (0,)), ((), ())), preferre...  48.6 us
    all_gather x1, waiting for transfers between devices, local(): lax.all_gather(source_decoder, 'layer', axis=0, tiled=True)  46.1 us
    all_to_all x1, waiting for transfers between devices, local(): lax.all_to_all(target_grads, 'feat', split_axis=1, concat_axis=0, tiled=T...  43.4 us
    all_gather x1, waiting for transfers between devices, local(): lax.all_gather(source_slab, 'layer', axis=0, tiled=True)  27.3 us
    all_to_all x1, blocking collectives, local(): lax.all_to_all(jnp.stack(jnp.split(source_acts, lax.axis_size('feat'), ax...  19.8 us
    dynamic_slice x24, local copies, waits for them, and re-layouts, one_pair(): target = targets[slot_pos]  14.1 us
  transfers between devices with their start and end apart: 3, of which 3 were waited for; matrix products, arithmetic and copies ran while one was open for 1% of the time, Pallas kernels for 0%

profile of v1, /device:TPU:5, one launch (start us, length us, event | category | flops | bytes accessed | tf_op | source)
XLA Modules:
  0.0 383.6 jit_solution(13111793089587479525)
XLA Ops:
  6.5 0.8 bitcast_dynamic-update-slice_fusion.7
  7.4 0.9 bitcast_dynamic-update-slice_fusion.6
  8.2 0.9 bitcast_dynamic-update-slice_fusion.5
  9.1 0.9 bitcast_dynamic-update-slice_fusion.4
  10.0 1.0 bitcast_dynamic-update-slice_fusion.3
  11.0 0.9 bitcast_dynamic-update-slice_fusion.2
  11.8 0.9 bitcast_dynamic-update-slice_fusion.1
  12.7 0.9 bitcast_dynamic-update-slice_fusion
  13.5 19.8 %all_to_all.24 = bf16[8,256,128]{2,1,0:T(8,128)(2,1)} all-to-all(bf16[8,256,128]{2,1,0:T(8,128)(2,1)S(1)} %bitcast_dynamic-update-slice_fusion), channel_id=1, replica_groups=mesh['layer'=4,'feat'=8] {'feat'}, dimensions={0} | all-to-all | bytes 1048576 | tf_op jit(solution)/shard_map/all_to_all | solution.py:12
  34.1 1.9 copy.12
  36.0 4.7 %all-to-all-start.1 = ((bf16[256,8,768]{2,0,1:T(8,128)(2,1)}), bf16[256,8,768]{2,0,1:T(8,128)(2,1)S(1)}, u32[]{:S(2)}, u32[]{:S(2)}) async-start(bf16[256,8,768]{2,0,1:T(8,128)(2,1)} %bitcast.40), calls=%async_computation.1 | async-start | bytes 6291456 | tf_op jit(solution)/shard_map/all_to_all | solution.py:17
  40.8 27.3 %all-gather.5.cloned.1.call-done = bf16[4,2048,128]{2,1,0:T(8,128)(2,1)} async-done(((bf16[1,2048,128]{2,1,0:T(8,128)(2,1)}), bf16[4,2048,128]{2,1,0:T(8,128)(2,1)}) %all-gather.5.cloned.1.call-update) | async-done | bytes 2097168 | tf_op jit(solution)/shard_map/all_gather | solution.py:28
  68.0 43.4 %all-to-all-done.1 = bf16[256,8,768]{2,0,1:T(8,128)(2,1)S(1)} async-done(((bf16[256,8,768]{2,0,1:T(8,128)(2,1)}), bf16[256,8,768]{2,0,1:T(8,128)(2,1)S(1)}, u32[]{:S(2)}, u32[]{:S(2)}) %all-to-all-start.1) | async-done | bytes 3145760 | tf_op jit(solution)/shard_map/all_to_all | solution.py:17
  111.4 46.1 %all-gather.3.cloned.1.call-done = bf16[4,128,8192]{2,1,0:T(8,128)(2,1)} async-done(((bf16[1,128,8192]{2,1,0:T(8,128)(2,1)}), bf16[4,128,8192]{2,1,0:T(8,128)(2,1)}) %all-gather.3.cloned.1.call-update) | async-done | bytes 8388624 | tf_op jit(solution)/shard_map/all_gather | solution.py:27
  157.5 1.3 broadcast_in_dim.10
  158.8 218.0 %while.10 = (s32[]{:T(128)}, f32[24,128,128]{2,1,0:T(8,128)}, s32[]{:T(128)}, s32[24]{0:T(128)S(1)}, bf16[4,128,8192]{2,1,0:T(8,128)(2,1)}, /*index=5*/s32[24]{0...) while((s32[]{:T(128)}, f32[24,128,128]{2,1,0:T(8,128)}, ...), condition=%wide.region_1.2_spmd, body=%wide.region_0.1_spmd.sunk | while | flops 335560704 | bytes 5439787 | solution.py:44
  162.9 2.9 fusion.21
  165.8 2.0 fusion.22
  172.0 2.9 fusion.21
  174.9 2.0 fusion.22
  181.0 2.9 fusion.21
  184.0 2.0 fusion.22
  190.1 2.9 fusion.21
  193.0 2.0 fusion.22
  199.1 2.9 fusion.21
  202.1 2.0 fusion.22
  208.2 2.9 fusion.21
  211.1 2.0 fusion.22
  217.2 2.9 fusion.21
  220.2 2.0 fusion.22
  226.3 2.9 fusion.21
  229.2 2.0 fusion.22
  235.4 2.9 fusion.21
  238.3 2.0 fusion.22
  244.4 2.9 fusion.21
  247.3 2.0 fusion.22
  253.5 2.9 fusion.21
  256.4 2.0 fusion.22
  262.5 2.9 fusion.21
  265.4 2.0 fusion.22
  271.6 2.9 fusion.21
  274.5 2.0 fusion.22
  280.6 2.9 fusion.21
  283.6 2.0 fusion.22
  289.7 2.9 fusion.21
  292.6 2.0 fusion.22
  298.7 2.9 fusion.21
  301.7 2.0 fusion.22
  307.8 2.9 fusion.21
  310.7 2.0 fusion.22
  316.8 2.9 fusion.21
  319.8 2.0 fusion.22
  325.9 2.9 fusion.21
  328.8 2.0 fusion.22
  335.0 2.9 fusion.21
  337.9 2.0 fusion.22
  344.0 2.9 fusion.21
  346.9 2.0 fusion.22
  353.1 2.9 fusion.21
  356.0 2.0 fusion.22
  362.1 2.9 fusion.21
  365.1 2.0 fusion.22
  371.2 2.9 fusion.21
  374.1 2.0 fusion.22
  (58 shorter events, 29.0 us)
Async XLA Ops:
  6.5 61.5 %all-gather.5.cloned.1.call-start = ((), (), s32[]{:S(2)}) async-start(), calls=%async_computation.3 | async-start | bytes 2621440 | tf_op jit(solution)/shard_map/all_gather | solution.py:28
  9.9 24.1 %copy-start = (bf16[256,6144]{1,0:T(8,128)(2,1)S(1)}, bf16[256,6144]{1,0:T(8,128)(2,1)}, u32[]{:S(2)}) copy-start(bf16[256,6144]{1,0:T(8,128)(2,1)} %param.12) | copy-start | bytes 9437188
  33.3 124.2 %all-gather.3.cloned.1.call-start = ((), (), s32[]{:S(2)}) async-start(), calls=%async_computation.2 | async-start | bytes 10485760 | tf_op jit(solution)/shard_map/all_gather | solution.py:27
  36.0 122.8 %copy-start.1 = (s32[1,1,24]{2,1,0:T(1,128)S(1)}, s32[1,1,24]{2,1,0:T(1,128)}, u32[]{:S(2)}) copy-start(s32[1,1,24]{2,1,0:T(1,128)} %param.13) | copy-start | bytes 292
  36.0 122.8 %copy-start.2 = (s32[1,1,24]{2,1,0:T(1,128)S(1)}, s32[1,1,24]{2,1,0:T(1,128)}, u32[]{:S(2)}) copy-start(s32[1,1,24]{2,1,0:T(1,128)} %param.14) | copy-start | bytes 292
  36.0 75.4 %all-to-all-start.1 = ((bf16[256,8,768]{2,0,1:T(8,128)(2,1)}), bf16[256,8,768]{2,0,1:T(8,128)(2,1)S(1)}, u32[]{:S(2)}, u32[]{:S(2)}) async-start(bf16[256,8,768]{2,0,1:T(8,128)(2,1)} %bitcast.40), calls=%async_computation.1 | async-start | bytes 6291456 | tf_op jit(solution)/shard_map/all_to_all | solution.py:17
Sparse Core Ops, SparseCore 0:
  33.4 34.5 all-gather.4
  69.8 87.5 all-gather.2
